TPU v7x, 32 devices: a whole 2x2x4 slice. The times are simulated.
32 devices in a mesh: dp: 8 (over z, core), mp: 4 (over y, x).
Axes of the slice: x: 2, y: 2, z: 4, core: 2. Of those that a mesh axis runs over, the one named last changes fastest.
Arguments:
- patches: bfloat16 [16, 1568, 1536], P('dp', 'mp'), parts along dimension 0, may hold values from -64 to 64
- visible: int32 [16, 157], P('dp'), parts along dimension 0, may hold values from 0 to 1567, as said below
- embed_weight: bfloat16 [1536, 6144], P(None, 'mp'), may hold values from -4 to 4
- embed_bias: bfloat16 [6144], P('mp'), may hold values from -3 to 3
- norm_gain: bfloat16 [6144], P('mp'), may hold values from 0.099609375 to 1.8984375
- qkv_weight: bfloat16 [6144, 3, 4096], P(None, None, 'mp'), may hold values from -0.078125 to 0.078125
- query_gain: float32 [4096], P('mp'), may hold values from 0.5 to 20
- key_gain: float32 [4096], P('mp'), may hold values from 0.5 to 20
Outputs:
- context: bfloat16 [16, 157, 4096], P('dp', None, 'mp'), parts along dimension 0
There are 8 independent parts, one for each index of `dp`. A program takes and returns all parts, laid end to end along the dimension named above; an argument that names none is the same for every part. Nothing has to cross between parts.
Inputs may be any that keep to these rules, and one draw needn't show every extreme that they name: `visible`: within a clip the entries are distinct; 0 and 1567 are among them.
All inputs are finite; a program needn't handle non-finite values.
Results may differ from a plain program's by a relative error of at most 0.033.
Values may be sent and summed in bfloat16 or wider, within the bound.
A program may use at most 192 MiB of HBM per device.

v0:
```python
import jax
import jax.numpy as jnp
from jax import lax
from jax.sharding import PartitionSpec as P

D = 6144
HS = 128


eps = 1e-06


def positions(index, columns):
    rate = jnp.power(jnp.float32(10000.0), -(2 * (columns // 2)).astype(jnp.float32) / D)
    angle = index.astype(jnp.float32)[..., None] * rate
    return jnp.where(columns % 2 == 0, jnp.sin(angle), jnp.cos(angle))


def normalize(values, gain):
    width = values.shape[-1]
    row_mean = jnp.sum(values, -1, keepdims=True) / width
    row_var = jnp.sum(values * values, -1, keepdims=True) / width - row_mean * row_mean
    return (values - row_mean) * lax.rsqrt(row_var + eps) * gain


def local(patches, visible, embed_weight, embed_bias, norm_gain, qkv_weight, query_gain, key_gain):
    clip_count, local_tubes, patch_width = patches.shape
    seen = visible.shape[1]
    row_count = clip_count * seen
    feature_local = embed_weight.shape[1]
    head_cols = qkv_weight.shape[2]
    heads_local = head_cols // HS
    first_tube = lax.axis_index("mp") * local_tubes
    selector = (
        visible[:, :, None] - first_tube == jnp.arange(local_tubes, dtype=jnp.int32)[None, None, :]
    ).astype(jnp.bfloat16)
    picked = (
        jnp.einsum("cvt,ctp->cvp", selector, patches, preferred_element_type=jnp.float32)
        .reshape(row_count, patch_width)
        .astype(jnp.bfloat16)
    )
    shared = lax.psum(picked, "mp").astype(jnp.float32).astype(jnp.bfloat16)
    embedded = jnp.dot(shared, embed_weight, preferred_element_type=jnp.float32)
    columns = lax.axis_index("mp") * feature_local + jnp.arange(feature_local, dtype=jnp.int32)
    placed = positions(visible, columns).reshape(row_count, feature_local)
    tokens = (embedded + embed_bias.astype(jnp.float32) + placed).astype(jnp.bfloat16)
    weight_flat = qkv_weight.reshape(qkv_weight.shape[0], 3 * head_cols)
    token_float = tokens.astype(jnp.float32)
    row_sums = lax.psum((jnp.sum(token_float, 1), jnp.sum(token_float * token_float, 1)), "mp")
    row_mean = row_sums[0] / D
    row_var = row_sums[1] / D - row_mean * row_mean
    normed = (
        (token_float - row_mean[:, None])
        * lax.rsqrt(row_var + eps)[:, None]
        * norm_gain.astype(jnp.float32)
    ).astype(jnp.bfloat16)
    projected = jnp.dot(
        lax.all_gather(normed, "mp", axis=1, tiled=True),
        weight_flat,
        preferred_element_type=jnp.float32,
    )
    projected = projected.astype(jnp.bfloat16).reshape(clip_count, seen, 3, heads_local, HS)
    queries = projected[:, :, 0].astype(jnp.float32)
    keys_local = projected[:, :, 1].astype(jnp.float32)
    values_local = projected[:, :, 2]
    query_normed = normalize(queries, query_gain.reshape(heads_local, HS)).astype(jnp.bfloat16)
    key_normed = normalize(keys_local, key_gain.reshape(heads_local, HS)).astype(jnp.bfloat16)
    scores = jnp.einsum(
        "cqhd,ckhd->chqk", query_normed, key_normed, preferred_element_type=jnp.float32
    ) / jnp.sqrt(jnp.float32(HS))
    probabilities = jax.nn.softmax(scores, axis=-1).astype(jnp.bfloat16)
    context = jnp.einsum(
        "chqk,ckhd->cqhd", probabilities, values_local, preferred_element_type=jnp.float32
    )
    return context.reshape(clip_count, seen, head_cols).astype(jnp.bfloat16)


def solution(mesh):
    return jax.shard_map(
        local,
        mesh=mesh,
        in_specs=(
            P("dp", "mp", None),
            P("dp", None),
            P(None, "mp"),
            P("mp"),
            P("mp"),
            P(None, None, "mp"),
            P("mp"),
            P("mp"),
        ),
        out_specs=P("dp", None, "mp"),
        check_vma=False,
    )
```

profile of v0, /device:TPU:0, one launch (start us, length us, event | category | flops | bytes accessed | tf_op | source)
XLA Modules:
  0.0 176.2 jit_solution(404531597808825003)
XLA Ops:
  6.5 0.9 fusion.50
  7.4 0.9 copy-done
  8.2 0.7 convolution_convert_fusion.1
  9.0 1.2 convert_element_type.68
  10.2 0.0 all-reduce.3.cloned.1.call-update
  10.2 0.0 all-gather.2.cloned.1.call-start
  10.3 0.1 mul.112
  10.4 54.4 %all-reduce.3.cloned.1.call-done = bf16[314,1536]{1,0:T(8,128)(2,1)} async-done(((bf16[314,1536]{1,0:T(8,128)(2,1)}), bf16[314,1536]{1,0:T(8,128)(2,1)}) %all-reduce.3.cloned.1.call-update) | async-done | bytes 964624 | tf_op jit(solution)/shard_map/psum | solution.py:42
  64.8 11.0 %convert_reduce_fusion = (f32[314]{0:T(512)S(1)}, f32[314]{0:T(512)S(1)}, bf16[314,1536]{1,0:T(8,128)(2,1)S(1)}) fusion(f32[1536]{0:T(1024)S(1)} %fusion.42, f32[314]{0:T(512)S(1)} %mul.112, pred[1536]{0:T(1024)(128)(4,1)S(1)} %fusion.37, f32[1536]{0:T(1024)S(1)} %convert_element_type.69, bf16[314,1536]{1,0:T(8,128)(2,1)} %all-reduce.3.cloned.1.call-done, ...), kind=kOutput, calls=%fused_computation.4 | convolution fusion | flops 1485978112 | bytes 6665400 | tf_op jit(solution)/shard_map/dot_general | solution.py:43
  75.8 9.1 %all-reduce = (f32[314]{0:T(512)S(1)}, f32[314]{0:T(512)S(1)}) all-reduce(f32[314]{0:T(512)S(1)} %get-tuple-element.6, f32[314]{0:T(512)S(1)} %get-tuple-element.5), channel_id=1, replica_groups=mesh['dp'=8,'mp'=4] {'mp'}, use_global_device_ids=true, to_apply=%region_4.5 | all-reduce | flops 628 | bytes 5024 | tf_op jit(solution)/shard_map/psum | solution.py:49
  84.9 1.4 fusion.9
  86.3 46.6 %copy.13 = bf16[6144,3,1024]{0,2,1:T(8,128)(2,1)} copy(bf16[6144,3,1024]{2,0,1:T(8,128)(2,1)} %param.13) | data formatting | bytes 75497472 | tf_op args[5]
  132.9 4.0 %all-gather.2.cloned.1.call-done = bf16[314,6144]{1,0:T(8,128)(2,1)} async-done(((bf16[314,1536]{1,0:T(8,128)(2,1)}), bf16[314,6144]{1,0:T(8,128)(2,1)}) %all-gather.2.cloned.1.call-update) | async-done | bytes 3858448 | tf_op jit(solution)/shard_map/all_gather | solution.py:58
  137.0 19.9 %convolution_convert_fusion = bf16[314,3072]{1,0:T(8,128)(2,1)} fusion(bf16[314,6144]{1,0:T(8,128)(2,1)} %all-gather.2.cloned.1.call-done, bf16[6144,3072]{0,1:T(8,128)(2,1)} %bitcast.51), kind=kOutput, calls=%fused_computation.1 | convolution fusion | flops 11854067712 | bytes 43536384 | tf_op jit(solution)/shard_map/dot_general | solution.py:57
  156.9 1.9 %copy.26 = bf16[40,8,24,128]{3,2,1,0:T(8,128)(2,1)S(1)} copy(bf16[40,8,24,128]{3,1,2,0:T(8,128)(2,1)} %bitcast.54) | data formatting | bytes 3932160
  158.8 0.3 slice.15
  159.1 0.3 fusion.49
  159.5 1.2 convert_reduce_fusion.1
  160.7 1.2 fusion.18
  161.9 2.9 %fusion.25 = f32[2,8,157,157]{2,3,1,0:T(8,128)S(1)} fusion(f32[8,128]{1,0:T(8,128)S(1)} %bitcast.55, f32[2,157,8]{1,2,0:T(8,128)S(1)} %get-tuple-element.15, f32[2,157,8]{1,2,0:T(8,128)S(1)} %get-tuple-element.14, f32[8,128]{1,0:T(8,128)S(1)} %bitcast.56, f32[2,157,8]{1,2,0:T(8,128)S(1)} %get-tuple-element.13, f32[2,157,8]{1,2,0:T(8,128)S(1)} %get-tuple-element.12, ...), kind=kOutput, calls=%fused_computation.39 | convolution fusion | flops 104177664 | bytes 2912064 | tf_op jit(solution)/shard_map/cqhd,ckhd->chqk/dot_general | solution.py:68
  164.8 2.5 %fusion.51 = (f32[2,8,157]{2,1,0:T(8,128)S(1)}, f32[2,8,157,157]{2,3,1,0:T(8,128)S(1)}) fusion(f32[2,8,157,157]{2,3,1,0:T(8,128)S(1)} %fusion.25), kind=kOutput, calls=%fused_computation.79 | output fusion | flops 1577692 | bytes 3165120 | tf_op jit(solution)/shard_map/sub | solution.py:71
  167.3 0.7 fusion.24
  168.1 0.3 copy.21
  168.4 1.0 reshape.88
  (20 shorter events, 0.1 us)
Async XLA Ops:
  6.5 1.7 copy-start
  6.5 58.3 %all-reduce.3.cloned.1.call-start = ((), (), s32[]{:S(2)}) async-start(), calls=%async_computation | async-start | bytes 1966080 | tf_op jit(solution)/shard_map/psum | solution.py:42
  9.0 1.4 copy-start.2
  9.0 1.4 copy-start.3
  10.2 126.8 %all-gather.2.cloned.1.call-start = ((), (), s32[]{:S(2)}) async-start(), calls=%async_computation.1 | async-start | bytes 4915200 | tf_op jit(solution)/shard_map/all_gather | solution.py:58
  159.5 2.4 %copy-start.4 = (f32[1024]{0:T(1024)S(1)}, f32[1024]{0:T(1024)}, u32[]{:S(2)}) copy-start(f32[1024]{0:T(1024)} %param.15) | copy-start | bytes 12292
  159.5 2.4 %copy-start.5 = (f32[1024]{0:T(1024)S(1)}, f32[1024]{0:T(1024)}, u32[]{:S(2)}) copy-start(f32[1024]{0:T(1024)} %param.14) | copy-start | bytes 12292
  167.3 2.0 %copy-start.1 = (bf16[2,392,1536]{2,1,0:T(8,128)(2,1)S(1)}, bf16[2,392,1536]{2,1,0:T(8,128)(2,1)}, u32[]{:S(2)}) copy-start(bf16[2,392,1536]{2,1,0:T(8,128)(2,1)} %param.8) | copy-start | bytes 7225348
Sparse Core Ops, SparseCore 0:
  10.5 54.2 all-reduce.2
  86.4 50.5 all-gather.1
where the time goes:
time: 178 us; the launch traced here: 176 us
  waiting for transfers between devices  58.5 us (33%)
  local copies, waits for them, and re-layouts  52.6 us (30%)
  matrix products  35.3 us (20%)
  between operations  13.6 us (8%)
  blocking collectives  9.11 us (5%)
  other arithmetic  7.1 us (4%)
    psum x1, waiting for transfers between devices, local(): shared = lax.psum(picked, 'mp').astype(jnp.float32).astype(jnp.bfloat16)  54.4 us
    unnamed x15, local copies, waits for them, and re-layouts  49.8 us
    dot_general x1, matrix products, local(): jnp.dot(lax.all_gather(normed, 'mp', axis=1, tiled=True), weight_flat, pr...  19.9 us
    dot_general x1, matrix products, local(): embedded = jnp.dot(shared, embed_weight, preferred_element_type=jnp.float32)  11 us
    psum x1, blocking collectives, local(): lax.psum((jnp.sum(token_float, 1), jnp.sum(token_float * token_float, 1))...  9.11 us
    all_gather x1, waiting for transfers between devices, local(): lax.all_gather(normed, 'mp', axis=1, tiled=True)  4.05 us
  transfers between devices with their start and end apart: 2, of which 2 were waited for; matrix products, arithmetic and copies ran while one was open for 27% of the time, Pallas kernels for 0%

commit v1 on v0

--- a/solution.py
+++ b/solution.py
@@ -1,6 +1,11 @@
+import functools
+
 import jax
 import jax.numpy as jnp
+import numpy as np
 from jax import lax
+from jax.experimental import pallas as pl
+from jax.experimental.pallas import tpu as pltpu
 from jax.sharding import PartitionSpec as P
 
 D = 6144
@@ -23,7 +28,7 @@
     return (values - row_mean) * lax.rsqrt(row_var + eps) * gain
 
 
-def local(patches, visible, embed_weight, embed_bias, norm_gain, qkv_weight, query_gain, key_gain):
+def local_generic(patches, visible, embed_weight, embed_bias, norm_gain, qkv_weight, query_gain, key_gain):
     clip_count, local_tubes, patch_width = patches.shape
     seen = visible.shape[1]
     row_count = clip_count * seen
@@ -75,7 +80,337 @@
     return context.reshape(clip_count, seen, head_cols).astype(jnp.bfloat16)
 
 
+MESH = pl.DeviceIdType.MESH
+NEG = -1e30
+
+
+def turn_table():
+    columns = np.arange(D)
+    turns = 10000.0 ** (-2.0 * (columns // 2) / D) / (2 * np.pi)
+    exponent = np.floor(np.log2(turns))
+    step = 2.0 ** (exponent - 11)
+    high = np.round(turns / step) * step
+    low = turns - high
+    phase = np.where(columns % 2 == 0, 0.0, 0.25)
+    table = np.zeros((8, D), np.float32)
+    table[0], table[1], table[2] = high, low, phase
+    return table
+
+
+def sine_of_turns(turn):
+    size = jnp.abs(turn)
+    size = jnp.minimum(size, 0.5 - size)
+    x = jnp.where(turn < 0, -size, size) * jnp.float32(2 * np.pi)
+    y = x * x
+    s = jnp.float32(2.7557319e-06) - jnp.float32(2.5052108e-08) * y
+    s = s * y - jnp.float32(1.9841270e-04)
+    s = s * y + jnp.float32(8.3333333e-03)
+    s = s * y - jnp.float32(1.6666667e-01)
+    return x + x * y * s
+
+
+def kernel(
+    sizes,
+    visible_ref, par_ref, table_ref, patches_hbm, embed_hbm, qkv_hbm,
+    out_ref,
+    patch, embed, weight, masked, part, picked, placed, tokens, stats, gains, normed, total,
+    local_sem, gain_send, gain_recv, part_send, part_recv, pick_send, pick_recv,
+    stat_send, stat_recv, token_send, token_recv,
+):
+    clips, rows, seen, quarter, width, heads = sizes
+    half = rows // 2
+    me = lax.axis_index("mp")
+    dp = lax.axis_index("dp")
+    xn = me + 1 - 2 * (me % 2)
+    yn = me + 2 - 4 * (me // 2)
+    dg = 3 - me
+    peers = (xn, yn, dg)
+
+    def push(src, dst, send, recv, peer):
+        return pltpu.make_async_remote_copy(
+            src_ref=src, dst_ref=dst, send_sem=send, recv_sem=recv,
+            device_id=(dp, peer), device_id_type=MESH,
+        )
+
+    patch_copies = [
+        pltpu.make_async_copy(patches_hbm.at[c], patch.at[c], local_sem.at[c]) for c in range(clips)
+    ]
+    embed_copy = pltpu.make_async_copy(embed_hbm, embed, local_sem.at[2])
+    for copy in patch_copies:
+        copy.start()
+    embed_copy.start()
+    barrier = pltpu.get_barrier_semaphore()
+    for peer in peers:
+        pl.semaphore_signal(barrier, inc=1, device_id=(dp, peer), device_id_type=MESH)
+    order = (me, xn, yn, dg)
+    weight_copies = []
+    for k, s in enumerate(order):
+        span = pl.ds(pl.multiple_of(s * width, width), width)
+        copy = pltpu.make_async_copy(
+            qkv_hbm.at[:, span, :], weight.at[:, span, :], local_sem.at[3 + k]
+        )
+        copy.start()
+        weight_copies.append(copy)
+    gains[me] = par_ref[1:2, :]
+
+    sends = []
+
+    def select(c):
+        patch_copies[c].wait()
+        tubes = patch.shape[1]
+        first = me * tubes
+        spot = lax.broadcasted_iota(jnp.int32, (rows, tubes), 1) + first
+        pick = (visible_ref[pl.ds(c * rows, rows), :] == spot).astype(jnp.float32).astype(jnp.bfloat16)
+        for q in range(4):
+            masked[c, q] = jnp.dot(
+                pick, patch[c, :, q * quarter:(q + 1) * quarter], preferred_element_type=jnp.float32
+            ).astype(jnp.bfloat16)
+
+    part_copies = [
+        [
+            push(masked.at[c, peer], part.at[c, k], part_send.at[c, k], part_recv.at[c, k], peer)
+            for k, peer in enumerate(peers)
+        ]
+        for c in range(clips)
+    ]
+
+    def spread(buffer, c, send, recv):
+        low, high = pl.ds(0, half), pl.ds(half, half)
+
+        def one(src, span, k, peer):
+            ref = buffer.at[c, src, span, :]
+            return push(ref, ref, send.at[c, k], recv.at[c, k], peer)
+
+        own = [one(me, low, 0, xn), one(me, high, 3, yn), one(me, high, 1, xn), one(me, low, 2, yn)]
+        forward = {0: one(xn, low, 4, yn), 3: one(yn, high, 5, xn)}
+        arrive = [
+            one(xn, low, 0, xn), one(xn, high, 1, xn), one(yn, low, 2, yn), one(yn, high, 3, yn),
+            one(dg, low, 4, yn), one(dg, high, 5, xn),
+        ]
+        return own, forward, arrive
+
+    pick_plan = [spread(picked, c, pick_send, pick_recv) for c in range(clips)]
+    token_plan = [spread(tokens, c, token_send, token_recv) for c in range(clips)]
+
+    def begin(plan):
+        for copy in plan[0]:
+            copy.start()
+
+    def relay(plan):
+        for k in (0, 3):
+            plan[2][k].wait_recv()
+            plan[1][k].start()
+
+    select(0)
+    pl.semaphore_wait(barrier, 3)
+    for copy in part_copies[0]:
+        copy.start()
+    gain_copies = [
+        push(gains.at[me], gains.at[me], gain_send.at[k], gain_recv.at[k], peer)
+        for k, peer in enumerate(peers)
+    ]
+    for copy in gain_copies:
+        copy.start()
+    select(1)
+    for copy in part_copies[1]:
+        copy.start()
+
+    here = pl.ds(pl.multiple_of(me * width, width), width)
+    for c in range(clips):
+        @pl.loop(0, rows // 16)
+        def _(r, c=c):
+            span = pl.ds(pl.multiple_of(r * 16, 16), 16)
+            vspan = pl.ds(pl.multiple_of(c * rows + r * 16, 16), 16)
+            index = visible_ref[vspan, :].astype(jnp.float32)
+            coarse = index * table_ref[0:1, here]
+            turn = (coarse - jnp.round(coarse)) + index * table_ref[1:2, here] + table_ref[2:3, here]
+            turn = turn - jnp.round(turn)
+            placed[c, span, :] = sine_of_turns(turn) + par_ref[0:1, :]
+
+    for c in range(clips):
+        for copy in part_copies[c]:
+            copy.wait_recv()
+        picked[c, me] = (masked[c, me] + part[c, 0]) + (part[c, 1] + part[c, 2])
+        begin(pick_plan[c])
+
+    ones = jnp.ones((8, width), jnp.bfloat16)
+    rowdims = (((1,), (1,)), ((), ()))
+    stat_copies = [
+        [
+            push(stats.at[c, me], stats.at[c, me], stat_send.at[c, k], stat_recv.at[c, k], peer)
+            for k, peer in enumerate(peers)
+        ]
+        for c in range(clips)
+    ]
+    for c in range(clips):
+        relay(pick_plan[c])
+        for k in (1, 2, 4, 5):
+            pick_plan[c][2][k].wait_recv()
+        if c == 0:
+            embed_copy.wait()
+        for n in range(width // 512):
+            cols = slice(n * 512, (n + 1) * 512)
+            value = placed[c, :, cols]
+            for q in range(4):
+                value += jnp.dot(
+                    picked[c, q], embed[q * quarter:(q + 1) * quarter, cols],
+                    preferred_element_type=jnp.float32,
+                )
+            tokens[c, me, :, cols] = value.astype(jnp.bfloat16)
+        begin(token_plan[c])
+        value = tokens[c, me]
+        wide = value.astype(jnp.float32)
+        square = wide * wide
+        top = square.astype(jnp.bfloat16)
+        rest = (square - top.astype(jnp.float32)).astype(jnp.bfloat16)
+        sums = lax.dot_general(ones, value, rowdims, preferred_element_type=jnp.float32)
+        squares = lax.dot_general(ones, top, rowdims, preferred_element_type=jnp.float32)
+        squares += lax.dot_general(ones, rest, rowdims, preferred_element_type=jnp.float32)
+        stats[c, me, 0:8, 0:rows] = sums
+        stats[c, me, 8:16, 0:rows] = squares
+        for copy in stat_copies[c]:
+            copy.start()
+
+    def row_stats(c):
+        for copy in stat_copies[c]:
+            copy.wait_recv()
+        both = (stats[c, 0] + stats[c, 1]) + (stats[c, 2] + stats[c, 3])
+        both = both[:, 0:rows]
+        mean = both[0:8, :] / D
+        scale = lax.rsqrt(both[8:16, :] / D - mean * mean + eps)
+        return jnp.transpose(mean)[:, 0:1], jnp.transpose(scale)[:, 0:1]
+
+    def project(c, k, mean, scale):
+        s = order[k]
+        normed[...] = (
+            (tokens[c, s].astype(jnp.float32) - mean) * scale * gains[s]
+        ).astype(jnp.bfloat16)
+        if c == 0:
+            weight_copies[k].wait()
+        span = pl.ds(pl.multiple_of(s * width, width), width)
+        block = 512
+        per = weight.shape[2] // block
+
+        @pl.loop(0, 3 * per)
+        def _(t):
+            j, n = t // per, t % per
+            cols = pl.ds(pl.multiple_of(n * block, block), block)
+            value = jnp.dot(normed[...], weight[j, span, cols], preferred_element_type=jnp.float32)
+            if k == 0:
+                total[c, j, :, cols] = value
+            else:
+                total[c, j, :, cols] += value
+
+    def head_norm(value, gain):
+        value = value.astype(jnp.bfloat16).astype(jnp.float32)
+        mean = jnp.sum(value, -1, keepdims=True) / HS
+        var = jnp.sum(value * value, -1, keepdims=True) / HS - mean * mean
+        return ((value - mean) * lax.rsqrt(var + eps) * gain).astype(jnp.bfloat16)
+
+    valid = lax.broadcasted_iota(jnp.int32, (rows, rows), 1) < seen
+
+    def attend(c):
+        for h in range(heads):
+            cols = slice(h * HS, (h + 1) * HS)
+            query = head_norm(total[c, 0, :, cols], par_ref[2:3, cols])
+            key = head_norm(total[c, 1, :, cols], par_ref[3:4, cols])
+            scores = lax.dot_general(query, key, rowdims, preferred_element_type=jnp.float32)
+            scores = jnp.where(valid, scores * jnp.float32(1 / np.sqrt(HS)), NEG)
+            weights = jnp.exp(scores - jnp.max(scores, -1, keepdims=True))
+            amount = jnp.sum(weights, -1, keepdims=True)
+            context = jnp.dot(
+                weights.astype(jnp.bfloat16), total[c, 2, :, cols].astype(jnp.bfloat16),
+                preferred_element_type=jnp.float32,
+            )
+            out_ref[c * rows:(c + 1) * rows, cols] = (context / amount).astype(jnp.bfloat16)
+
+    for copy in gain_copies:
+        copy.wait_recv()
+    mean0, scale0 = row_stats(0)
+    project(0, 0, mean0, scale0)
+    relay(token_plan[0])
+    token_plan[0][2][1].wait_recv()
+    project(0, 1, mean0, scale0)
+    token_plan[0][2][2].wait_recv()
+    project(0, 2, mean0, scale0)
+    mean1, scale1 = row_stats(1)
+    project(1, 0, mean1, scale1)
+    token_plan[0][2][4].wait_recv()
+    token_plan[0][2][5].wait_recv()
+    project(0, 3, mean0, scale0)
+    relay(token_plan[1])
+    attend(0)
+    token_plan[1][2][1].wait_recv()
+    project(1, 1, mean1, scale1)
+    token_plan[1][2][2].wait_recv()
+    project(1, 2, mean1, scale1)
+    token_plan[1][2][4].wait_recv()
+    token_plan[1][2][5].wait_recv()
+    project(1, 3, mean1, scale1)
+    attend(1)
+
+    for copy in gain_copies:
+        copy.wait_send()
+    for c in range(clips):
+        for copy in part_copies[c] + stat_copies[c]:
+            copy.wait_send()
+        for plan in (pick_plan[c], token_plan[c]):
+            for copy in plan[0] + [plan[1][0], plan[1][3]]:
+                copy.wait_send()
+
+
+def local_square(patches, visible, embed_weight, embed_bias, norm_gain, qkv_weight, query_gain, key_gain):
+    clips, tubes, patch_width = patches.shape
+    seen = visible.shape[1]
+    rows = -(-seen // 32) * 32
+    quarter = patch_width // 4
+    width = embed_weight.shape[1]
+    head_cols = qkv_weight.shape[2]
+    heads = head_cols // HS
+    index = jnp.pad(visible, ((0, 0), (0, rows - seen)), constant_values=-1).reshape(clips * rows, 1)
+    f32 = jnp.float32
+    par = jnp.stack(
+        [
+            embed_bias.astype(f32), norm_gain.astype(f32),
+            jnp.pad(query_gain, (0, width - head_cols)), jnp.pad(key_gain, (0, width - head_cols)),
+        ]
+    )
+    vmem = pl.BlockSpec(memory_space=pltpu.VMEM)
+    hbm = pl.BlockSpec(memory_space=pl.ANY)
+    bf16 = jnp.bfloat16
+    dma = pltpu.SemaphoreType.DMA
+    out = pl.pallas_call(
+        functools.partial(kernel, (clips, rows, seen, quarter, width, heads)),
+        out_shape=jax.ShapeDtypeStruct((clips * rows, head_cols), bf16),
+        in_specs=[vmem, vmem, vmem, hbm, hbm, hbm],
+        out_specs=vmem,
+        scratch_shapes=[
+            pltpu.VMEM((clips, tubes, patch_width), bf16),
+            pltpu.VMEM((patch_width, width), bf16),
+            pltpu.VMEM((3, D, head_cols), bf16),
+            pltpu.VMEM((clips, 4, rows, quarter), bf16),
+            pltpu.VMEM((clips, 3, rows, quarter), bf16),
+            pltpu.VMEM((clips, 4, rows, quarter), bf16),
+            pltpu.VMEM((clips, rows, width), f32),
+            pltpu.VMEM((clips, 4, rows, width), bf16),
+            pltpu.VMEM((clips, 4, 16, 256), f32),
+            pltpu.VMEM((4, 1, width), f32),
+            pltpu.VMEM((rows, width), bf16),
+            pltpu.VMEM((clips, 3, rows, head_cols), f32),
+            dma((7,)), dma((3,)), dma((3,)), dma((clips, 3)), dma((clips, 3)),
+            dma((clips, 6)), dma((clips, 6)), dma((clips, 3)), dma((clips, 3)),
+            dma((clips, 6)), dma((clips, 6)),
+        ],
+        compiler_params=pltpu.CompilerParams(
+            collective_id=0, has_side_effects=True, vmem_limit_bytes=63 * 1024 * 1024
+        ),
+        name="encoder_block",
+    )(index, par, jnp.asarray(turn_table()), patches, embed_weight, jnp.transpose(qkv_weight, (1, 0, 2)))
+    return out.reshape(clips, rows, head_cols)[:, :seen]
+
+
 def solution(mesh):
+    local = local_square if mesh.shape["mp"] == 4 else local_generic
     return jax.shard_map(
         local,
         mesh=mesh,

time: 178 us -> 81.4 us (0.46)
  Pallas kernels: 0 us -> 73.5 us
  waiting for transfers between devices: 58.5 us -> 0 us
  local copies, waits for them, and re-layouts: 52.6 us -> 6.92 us
  matrix products: 35.3 us -> 0 us
  between operations: 13.6 us -> 0.01 us
  blocking collectives: 9.11 us -> 0 us
  other arithmetic: 7.1 us -> 0.62 us
    pallas_call x0 -> x1, Pallas kernels: none -> 73.5 us  [local_square(): pl.pallas_call(functools.partial(kernel, (clips, rows, seen, quarter, wid...]
    psum x1 -> x0, waiting for transfers between devices: 54.4 us -> none  [local(): shared = lax.psum(picked, 'mp').astype(jnp.float32).astype(jnp.bfloat16)]
    unnamed x15 -> x1, local copies, waits for them, and re-layouts: 49.8 us -> 2.58 us
    dot_general x5 -> x0, matrix products: 35.3 us -> none  [the longest x1 19.9 us: local(): jnp.dot(lax.all_gather(normed, 'mp', axis=1, tiled=True), weight_flat, pr...]
    psum x1 -> x0, blocking collectives: 9.11 us -> none  [local(): lax.psum((jnp.sum(token_float, 1), jnp.sum(token_float * token_float, 1))...]
    all_gather x1 -> x0, waiting for transfers between devices: 4.05 us -> none  [local(): lax.all_gather(normed, 'mp', axis=1, tiled=True)]
    sub x1 -> x0, other arithmetic: 2.48 us -> none  [local(): probabilities = jax.nn.softmax(scores, axis=-1).astype(jnp.bfloat16)]
    convert_element_type x3 -> x0, local copies, waits for them, and re-layouts: 2.41 us -> none  [the longest x2 1.23 us: local(): return context.reshape(clip_count, seen, head_cols).astype(jnp.bfloat16)]
  transfers between devices with their start and end apart: 2 -> 0, of which waited for: 2 -> 0; matrix products, arithmetic and copies ran while one was open for 27% -> 0% of each run, Pallas kernels for 0% -> 0%
where the time goes in v1:
time: 81.4 us; the launch traced here: 81 us
  Pallas kernels  73.5 us (90%)
  local copies, waits for them, and re-layouts  6.92 us (9%)
    pallas_call x1, Pallas kernels, local_square(): pl.pallas_call(functools.partial(kernel, (clips, rows, seen, quarter, wid...  73.5 us
    unnamed x1, local copies, waits for them, and re-layouts  2.58 us

profile of v1, /device:TPU:0, one launch (start us, length us, event | category | flops | bytes accessed | tf_op | source)
XLA Modules:
  0.0 81.0 jit_solution(5694492451873419017)
XLA Ops:
  0.0 0.7 pad.11
  0.7 0.7 reshape.8
  1.4 0.7 reshape.9
  2.1 0.7 pad.12
  2.8 0.7 pad.13
  3.5 0.6 pad_maximum_fusion.par_ref
  4.1 0.9 %reshape.10.visible_ref = s32[320,1]{1,0:T(8,128)} reshape(s32[2,160]{1,0:T(2,128)S(1)} %pad.11) | data formatting | bytes 2560 | tf_op jit(solution)/shard_map/reshape | solution.py:370
  5.0 73.5 %encoder_block.1 = bf16[320,1024]{1,0:T(8,128)(2,1)} custom-call(s32[320,1]{1,0:T(8,128)} %reshape.10.visible_ref, f32[4,1536]{1,0:T(4,128)} %pad_maximum_fusion.par_ref, f32[8,6144]{1,0:T(8,128)} %constant.7.clone.table_ref, bf16[2,392,1536]{2,1,0:T(8,128)(2,1)} %patches_hbm.1, bf16[1536,1536]{1,0:T(8,128)(2,1)} %embed_hbm.1, bf16[3,6144,1024]{2,1,0:T(8,128)(2,1)} %bitcast.3), custom_call_target="tpu_custom_call" | custom-call | tf_op jit(solution)/shard_map/encoder_block/pallas_call | solution.py:382
  78.5 2.6 %copy.13 = bf16[2,157,1024]{2,0,1:T(2,128)(2,1)} copy(bf16[2,157,1024]{2,1,0:T(8,128)(2,1)} %bitcast.4) | data formatting | bytes 1286144
  (2 shorter events, 0.0 us)

commit v2 on v1

--- a/solution.py
+++ b/solution.py
@@ -111,9 +111,9 @@
 
 def kernel(
     sizes,
-    visible_ref, par_ref, table_ref, patches_hbm, embed_hbm, qkv_hbm,
+    visible_ref, bias_ref, gain_ref, query_gain_ref, key_gain_ref, table_ref, patches_hbm, embed_hbm, qkv_hbm,
     out_ref,
-    patch, embed, weight, masked, part, picked, placed, tokens, stats, gains, normed, total,
+    patch, embed, weight, masked, part, picked, placed, tokens, stats, gains, normed, total, line, index_ref, hop,
     local_sem, gain_send, gain_recv, part_send, part_recv, pick_send, pick_recv,
     stat_send, stat_recv, token_send, token_recv,
 ):
@@ -151,7 +151,15 @@
         )
         copy.start()
         weight_copies.append(copy)
-    gains[me] = par_ref[1:2, :]
+    bias = bias_ref[...].astype(jnp.float32).reshape(1, width)
+    query_gain = query_gain_ref[...].reshape(1, heads * HS)
+    key_gain = key_gain_ref[...].reshape(1, heads * HS)
+    gains[me] = gain_ref[...].astype(jnp.float32).reshape(1, width)
+    line[...] = jnp.full(line.shape, -1.0, jnp.float32)
+    line[0:clips, 0:seen] = visible_ref[...].astype(jnp.float32)
+    upright = jnp.transpose(line[...])
+    for c in range(clips):
+        index_ref[c * rows:(c + 1) * rows, :] = upright[0:rows, c:c + 1]
 
     sends = []
 
@@ -159,24 +167,39 @@
         patch_copies[c].wait()
         tubes = patch.shape[1]
         first = me * tubes
-        spot = lax.broadcasted_iota(jnp.int32, (rows, tubes), 1) + first
-        pick = (visible_ref[pl.ds(c * rows, rows), :] == spot).astype(jnp.float32).astype(jnp.bfloat16)
+        spot = (lax.broadcasted_iota(jnp.int32, (rows, tubes), 1) + first).astype(jnp.float32)
+        pick = (index_ref[pl.ds(c * rows, rows), :] == spot).astype(jnp.float32).astype(jnp.bfloat16)
         for q in range(4):
             masked[c, q] = jnp.dot(
                 pick, patch[c, :, q * quarter:(q + 1) * quarter], preferred_element_type=jnp.float32
             ).astype(jnp.bfloat16)
 
-    part_copies = [
-        [
-            push(masked.at[c, peer], part.at[c, k], part_send.at[c, k], part_recv.at[c, k], peer)
-            for k, peer in enumerate(peers)
+    low, high = pl.ds(0, half), pl.ds(half, half)
+
+    def gather_parts(c):
+        def one(k, peer, src, dst):
+            return push(src, dst, part_send.at[c, k], part_recv.at[c, k], peer)
+
+        return [
+            one(0, xn, masked.at[c, dg, low, :], hop.at[c, 0]),
+            one(1, yn, masked.at[c, dg, high, :], hop.at[c, 1]),
+            one(2, xn, masked.at[c, xn, low, :], part.at[c, 0, low, :]),
+            one(3, yn, masked.at[c, yn, high, :], part.at[c, 1, high, :]),
+            one(4, xn, masked.at[c, xn, high, :], part.at[c, 0, high, :]),
+            one(5, yn, masked.at[c, yn, low, :], part.at[c, 1, low, :]),
         ]
-        for c in range(clips)
-    ]
+
+    part_copies = [gather_parts(c) for c in range(clips)]
+
+    def merge(c):
+        part_copies[c][0].wait_recv()
+        masked[c, yn, 0:half, :] = masked[c, yn, 0:half, :] + hop[c, 0]
+        part_copies[c][5].start()
+        part_copies[c][1].wait_recv()
+        masked[c, xn, half:rows, :] = masked[c, xn, half:rows, :] + hop[c, 1]
+        part_copies[c][4].start()
 
     def spread(buffer, c, send, recv):
-        low, high = pl.ds(0, half), pl.ds(half, half)
-
         def one(src, span, k, peer):
             ref = buffer.at[c, src, span, :]
             return push(ref, ref, send.at[c, k], recv.at[c, k], peer)
@@ -203,7 +226,7 @@
 
     select(0)
     pl.semaphore_wait(barrier, 3)
-    for copy in part_copies[0]:
+    for copy in part_copies[0][0:4]:
         copy.start()
     gain_copies = [
         push(gains.at[me], gains.at[me], gain_send.at[k], gain_recv.at[k], peer)
@@ -212,26 +235,33 @@
     for copy in gain_copies:
         copy.start()
     select(1)
-    for copy in part_copies[1]:
+    for copy in part_copies[1][0:4]:
         copy.start()
 
     here = pl.ds(pl.multiple_of(me * width, width), width)
-    for c in range(clips):
+    def place(c):
         @pl.loop(0, rows // 16)
-        def _(r, c=c):
+        def _(r):
             span = pl.ds(pl.multiple_of(r * 16, 16), 16)
             vspan = pl.ds(pl.multiple_of(c * rows + r * 16, 16), 16)
-            index = visible_ref[vspan, :].astype(jnp.float32)
+            index = index_ref[vspan, :]
             coarse = index * table_ref[0:1, here]
             turn = (coarse - jnp.round(coarse)) + index * table_ref[1:2, here] + table_ref[2:3, here]
             turn = turn - jnp.round(turn)
-            placed[c, span, :] = sine_of_turns(turn) + par_ref[0:1, :]
-
-    for c in range(clips):
-        for copy in part_copies[c]:
+            placed[c, span, :] = sine_of_turns(turn) + bias
+
+    def collect(c):
+        for copy in part_copies[c][2:6]:
             copy.wait_recv()
-        picked[c, me] = (masked[c, me] + part[c, 0]) + (part[c, 1] + part[c, 2])
+        picked[c, me] = masked[c, me] + part[c, 0] + part[c, 1]
         begin(pick_plan[c])
+
+    merge(0)
+    place(0)
+    merge(1)
+    collect(0)
+    place(1)
+    collect(1)
 
     ones = jnp.ones((8, width), jnp.bfloat16)
     rowdims = (((1,), (1,)), ((), ()))
@@ -312,8 +342,8 @@
     def attend(c):
         for h in range(heads):
             cols = slice(h * HS, (h + 1) * HS)
-            query = head_norm(total[c, 0, :, cols], par_ref[2:3, cols])
-            key = head_norm(total[c, 1, :, cols], par_ref[3:4, cols])
+            query = head_norm(total[c, 0, :, cols], query_gain[:, cols])
+            key = head_norm(total[c, 1, :, cols], key_gain[:, cols])
             scores = lax.dot_general(query, key, rowdims, preferred_element_type=jnp.float32)
             scores = jnp.where(valid, scores * jnp.float32(1 / np.sqrt(HS)), NEG)
             weights = jnp.exp(scores - jnp.max(scores, -1, keepdims=True))
@@ -337,8 +367,8 @@
     project(1, 0, mean1, scale1)
     token_plan[0][2][4].wait_recv()
     token_plan[0][2][5].wait_recv()
+    relay(token_plan[1])
     project(0, 3, mean0, scale0)
-    relay(token_plan[1])
     attend(0)
     token_plan[1][2][1].wait_recv()
     project(1, 1, mean1, scale1)
@@ -367,14 +397,7 @@
     width = embed_weight.shape[1]
     head_cols = qkv_weight.shape[2]
     heads = head_cols // HS
-    index = jnp.pad(visible, ((0, 0), (0, rows - seen)), constant_values=-1).reshape(clips * rows, 1)
     f32 = jnp.float32
-    par = jnp.stack(
-        [
-            embed_bias.astype(f32), norm_gain.astype(f32),
-            jnp.pad(query_gain, (0, width - head_cols)), jnp.pad(key_gain, (0, width - head_cols)),
-        ]
-    )
     vmem = pl.BlockSpec(memory_space=pltpu.VMEM)
     hbm = pl.BlockSpec(memory_space=pl.ANY)
     bf16 = jnp.bfloat16
@@ -382,14 +405,14 @@
     out = pl.pallas_call(
         functools.partial(kernel, (clips, rows, seen, quarter, width, heads)),
         out_shape=jax.ShapeDtypeStruct((clips * rows, head_cols), bf16),
-        in_specs=[vmem, vmem, vmem, hbm, hbm, hbm],
+        in_specs=[vmem] * 6 + [hbm] * 3,
         out_specs=vmem,
         scratch_shapes=[
             pltpu.VMEM((clips, tubes, patch_width), bf16),
             pltpu.VMEM((patch_width, width), bf16),
             pltpu.VMEM((3, D, head_cols), bf16),
             pltpu.VMEM((clips, 4, rows, quarter), bf16),
-            pltpu.VMEM((clips, 3, rows, quarter), bf16),
+            pltpu.VMEM((clips, 2, rows, quarter), bf16),
             pltpu.VMEM((clips, 4, rows, quarter), bf16),
             pltpu.VMEM((clips, rows, width), f32),
             pltpu.VMEM((clips, 4, rows, width), bf16),
@@ -397,7 +420,10 @@
             pltpu.VMEM((4, 1, width), f32),
             pltpu.VMEM((rows, width), bf16),
             pltpu.VMEM((clips, 3, rows, head_cols), f32),
-            dma((7,)), dma((3,)), dma((3,)), dma((clips, 3)), dma((clips, 3)),
+            pltpu.VMEM((8, -(-rows // 128) * 128), f32),
+            pltpu.VMEM((clips * rows, 1), f32),
+            pltpu.VMEM((clips, 2, rows // 2, quarter), bf16),
+            dma((7,)), dma((3,)), dma((3,)), dma((clips, 6)), dma((clips, 6)),
             dma((clips, 6)), dma((clips, 6)), dma((clips, 3)), dma((clips, 3)),
             dma((clips, 6)), dma((clips, 6)),
         ],
@@ -405,7 +431,10 @@
             collective_id=0, has_side_effects=True, vmem_limit_bytes=63 * 1024 * 1024
         ),
         name="encoder_block",
-    )(index, par, jnp.asarray(turn_table()), patches, embed_weight, jnp.transpose(qkv_weight, (1, 0, 2)))
+    )(
+        visible, embed_bias, norm_gain, query_gain, key_gain, jnp.asarray(turn_table()), patches, embed_weight,
+        jnp.transpose(qkv_weight, (1, 0, 2)),
+    )
     return out.reshape(clips, rows, head_cols)[:, :seen]
 
 

time: 81.4 us -> 73.5 us (0.903)
  local copies, waits for them, and re-layouts: 6.92 us -> 2.58 us
  Pallas kernels: 73.5 us -> 70.8 us
    pallas_call x1, Pallas kernels: 73.5 us -> 70.8 us  [local_square(): pl.pallas_call(functools.partial(kernel, (clips, rows, seen, quarter, wid...]
    pad x3 -> x0, local copies, waits for them, and re-layouts: 2.06 us -> none  [the longest x1 0.69 us: local_square(): jnp.pad(key_gain, (0, width - head_cols))]
    another operation x4 -> x0, local copies, waits for them, and re-layouts: 1.4 us -> none  [local_square(): jnp.stack([embed_bias.astype(f32), norm_gain.astype(f32), jnp.pad(query_g...]
    reshape x1 -> x0, local copies, waits for them, and re-layouts: 0.87 us -> none  [local_square(): jnp.pad(visible, ((0, 0), (0, rows - seen)), constant_values=-1)]
where the time goes in v2:
time: 73.5 us; the launch traced here: 73.4 us
  Pallas kernels  70.8 us (96%)
  local copies, waits for them, and re-layouts  2.58 us (4%)
    pallas_call x1, Pallas kernels, local_square(): pl.pallas_call(functools.partial(kernel, (clips, rows, seen, quarter, wid...  70.8 us
    unnamed x1, local copies, waits for them, and re-layouts  2.58 us

profile of v2, /device:TPU:0, one launch (start us, length us, event | category | flops | bytes accessed | tf_op | source)
XLA Modules:
  0.0 73.4 jit_solution(14847410940913831021)
XLA Ops:
  0.0 70.8 %encoder_block.1 = bf16[320,1024]{1,0:T(8,128)(2,1)} custom-call(s32[2,157]{1,0:T(2,128)} %visible_ref.1, bf16[1536]{0:T(1024)(128)(2,1)} %bias_ref.1, bf16[1536]{0:T(1024)(128)(2,1)} %gain_ref.1, f32[1024]{0:T(1024)} %query_gain_ref.1, f32[1024]{0:T(1024)} %key_gain_ref.1, f32[8,6144]{1,0:T(8,128)} %constant.2.clone.table_ref, ...), custom_call_target="tpu_custom_call" | custom-call | tf_op jit(solution)/shard_map/encoder_block/pallas_call | solution.py:405
  70.8 2.6 %copy.11 = bf16[2,157,1024]{2,0,1:T(2,128)(2,1)} copy(bf16[2,157,1024]{2,1,0:T(8,128)(2,1)} %bitcast.4) | data formatting | bytes 1286144
